TPU v7x, 256 devices: a whole 4x4x8 slice. The times are simulated.
256 devices in a mesh: gy: 32 (over z_hi, y, x), gz: 8 (over z_lo, core).
Axes of the slice: x: 4, y: 4, z: 8 (z_hi: 2, z_lo: 4; z = z_hi * 4 + z_lo), core: 2. Of those that a mesh axis runs over, the one named last changes fastest.
Arguments:
- kspace: float32 [2, 4, 256, 32, 256], P(None, None, 'gy', 'gz'), may hold values from -6 to 6
- cotangent: float32 [2, 4, 256, 32, 256], P(None, None, 'gy', 'gz'), may hold values from -6 to 6
- weight_in: bfloat16 [16, 8, 3, 3, 3], replicated, may hold values from -0.4375 to 0.4375
- weight_out: bfloat16 [8, 16, 3, 3, 3], replicated, may hold values from -0.3125 to 0.3125
- consistency_weight: float32 [1], replicated, may hold values from 0.2 to 1
- sampling_mask: int32 [256, 32], P('gy', 'gz'), may hold values 0 or 1
Outputs:
- grad_kspace: float32 [2, 4, 256, 32, 256], P(None, None, 'gy', 'gz')
- grad_weight_in: float32 [16, 8, 3, 3, 3], replicated
- grad_weight_out: float32 [8, 16, 3, 3, 3], replicated
Inputs may be any that keep to these rules, and one draw needn't show every extreme that they name: `sampling_mask`: 1 marks a sampled phase-encode line.
All inputs are finite; a program needn't handle non-finite values. No bound on the sum of `sampling_mask` on one device may be relied on, other than what follows from the above.
Results may differ from a plain program's by a relative error of at most 0.0059.
Values may be sent and summed in bfloat16 or wider, within the bound.
A program may use at most 128 MiB of HBM per device.

v0:
```python
import math
import jax
import jax.numpy as jnp
from jax import lax
from jax.sharding import PartitionSpec as P


def as_sent(shard):
    return jax.tree.map(lambda a: a.astype(jnp.bfloat16) if a.dtype == jnp.float32 else a, shard)


def extended(shard, sides, width):
    for axis, dim in sides:
        count, length = (lax.axis_size(axis), shard.shape[dim])
        up = [(i, (i + 1) % count) for i in range(count - 1)]
        down = [(j, i) for i, j in up]
        last = lax.slice_in_dim(shard, length - width, length, axis=dim)
        first = lax.slice_in_dim(shard, 0, width, axis=dim)
        before = lax.ppermute(last, axis, up)
        after = lax.ppermute(first, axis, down)
        shard = jnp.concatenate([before, shard, after], axis=dim)
    return shard


def dft_table(length, direction):
    indices = lax.iota(jnp.int32, length)
    products = indices[:, None] * indices[None, :] % length
    phases = products.astype(jnp.float32) * (2.0 * math.pi / length)
    cosine = jnp.cos(phases) / math.sqrt(length)
    sine_part = direction * jnp.sin(phases) / math.sqrt(length)
    return jnp.stack([jnp.stack([cosine, -sine_part]), jnp.stack([sine_part, cosine])])


def spectral(spectrum, direction):
    field_parts = spectrum.shape[1]
    cells_y = spectrum.shape[2]
    cells_z = spectrum.shape[3]
    readout = spectrum.shape[4]
    length_y = cells_y * lax.axis_size("gy")
    length_z = cells_z * lax.axis_size("gz")
    table_y = dft_table(length_y, direction)
    table_z = dft_table(length_z, direction)
    flattened = spectrum.reshape(2, field_parts, cells_y, cells_z * readout)
    transformed_y = jnp.einsum(
        "pqvy,qcym->pcvm",
        table_y,
        lax.all_to_all(flattened, "gy", split_axis=3, concat_axis=2, tiled=True),
        precision=lax.Precision.HIGHEST,
    )
    turned_field = lax.all_to_all(
        lax.all_to_all(transformed_y, "gy", split_axis=2, concat_axis=3, tiled=True),
        "gz",
        split_axis=2,
        concat_axis=3,
        tiled=True,
    )
    shaped = turned_field.reshape(
        turned_field.shape[0], turned_field.shape[1], turned_field.shape[2], length_z, readout
    )
    turned = jnp.einsum("pqwz,qcyzx->pcywx", table_z, shaped, precision=lax.Precision.HIGHEST)
    transformed_z = turned.reshape(turned_field.shape)
    result = lax.all_to_all(
        as_sent(transformed_z), "gz", split_axis=3, concat_axis=2, tiled=True
    ).astype(transformed_z.dtype)
    return result.reshape(spectrum.shape)


def with_rims(volume):
    return extended(volume, (("gy", 2), ("gz", 3)), 1)


def convolve(padded, kernel):
    return lax.conv_general_dilated(
        padded,
        kernel,
        (1, 1, 1),
        ((0, 0), (0, 0), (1, 1)),
        dimension_numbers=("NCDHW", "OIDHW", "NCDHW"),
        preferred_element_type=jnp.float32,
    )


def kernel_gradient(padded, cotangent_part):
    summed = lax.conv_general_dilated(
        padded,
        cotangent_part,
        (1, 1, 1),
        ((0, 0), (0, 0), (1, 1)),
        dimension_numbers=("CNDHW", "IODHW", "NCDHW"),
        preferred_element_type=jnp.float32,
    )
    return summed.transpose(1, 0, 2, 3, 4)


def flipped(kernel):
    return jnp.flip(kernel, (2, 3, 4)).transpose(1, 0, 2, 3, 4)


def local(kspace, cotangent, weight_in, weight_out, consistency_weight, sampling_mask):
    coil_count = kspace.shape[1]
    channels = 2 * coil_count
    cells_y = kspace.shape[2]
    cells_z = kspace.shape[3]
    readout = kspace.shape[4]
    voxels = readout * cells_y * cells_z * lax.axis_size("gy") * lax.axis_size("gz")
    image_field = spectral(kspace, 1.0)
    back_field = spectral(cotangent, 1.0)
    image_in = image_field.astype(jnp.bfloat16).reshape(1, channels, cells_y, cells_z, readout)
    back_out = (-back_field).astype(jnp.bfloat16).reshape(1, channels, cells_y, cells_z, readout)
    image_padded = with_rims(image_in)
    back_padded = with_rims(back_out)
    hidden = convolve(image_padded, weight_in)
    active = jax.nn.silu(hidden).astype(jnp.bfloat16)
    active_padded = with_rims(active)
    local_out = kernel_gradient(active_padded, back_out)
    back_active = convolve(back_padded, flipped(weight_out))
    gate = jax.nn.sigmoid(hidden)
    back_hidden = (back_active * gate * (1.0 + hidden * (1.0 - gate))).astype(jnp.bfloat16)
    local_in = kernel_gradient(image_padded, back_hidden)
    hidden_padded = with_rims(back_hidden)
    back_image = convolve(hidden_padded, flipped(weight_in))
    spectrum = spectral(back_image.reshape(2, coil_count, cells_y, cells_z, readout), -1.0)
    summed_in, summed_out = lax.psum((local_in, local_out), ("gy", "gz"))
    scale = 1.0 / math.sqrt(voxels)
    mask_field = sampling_mask.astype(jnp.float32)[None, None, :, :, None]
    grad_kspace = cotangent - consistency_weight[0] * mask_field * cotangent + spectrum
    return (grad_kspace, summed_in * scale, summed_out * scale)


def solution(mesh):
    placed = (
        P(None, None, "gy", "gz", None),
        P(None, None, "gy", "gz", None),
        P(),
        P(),
        P(),
        P("gy", "gz"),
    )
    return jax.shard_map(
        local,
        mesh=mesh,
        in_specs=placed,
        out_specs=(P(None, None, "gy", "gz", None), P(), P()),
        check_vma=False,
    )
```

profile of v0, /device:TPU:1, one launch (start us, length us, event | category | flops | bytes accessed | tf_op | source)
XLA Modules:
  0.0 722.7 jit_solution(2760864033944492216)
XLA Ops:
  0.7 4.5 copy.348
  5.2 6.9 reshape.431
  12.1 14.5 %all-to-all-start.4 = ((f32[32,1,2048]{2,1,0:T(1,128)}), f32[32,1,2048]{2,1,0:T(1,128)S(1)}, u32[]{:S(2)}, u32[]{:S(2)}) async-start(f32[32,1,2048]{2,1,0:T(1,128)} %reshape.431), calls=%async_computation.4 | async-start | bytes 524288 | tf_op jit(solution)/shard_map/all_to_all | solution.py:47
  29.7 6.9 reshape.437
  38.5 11.0 %all-to-all-start = ((f32[32,1,2048]{2,1,0:T(1,128)}), f32[32,1,2048]{2,1,0:T(1,128)S(1)}, u32[]{:S(2)}, u32[]{:S(2)}) async-start(f32[32,1,2048]{2,1,0:T(1,128)} %reshape.437), calls=%async_computation | async-start | bytes 524288 | tf_op jit(solution)/shard_map/all_to_all | solution.py:47
  54.6 6.3 reshape.432
  60.9 3.5 copy.417
  68.4 12.0 %all-to-all-start.5 = ((f32[32,1,2048]{2,1,0:T(1,128)}), f32[32,1,2048]{2,1,0:T(1,128)S(1)}, u32[]{:S(2)}, u32[]{:S(2)}) async-start(f32[32,1,2048]{2,1,0:T(1,128)} %reshape.433), calls=%async_computation.5 | async-start | bytes 524288 | tf_op jit(solution)/shard_map/all_to_all | solution.py:51
  81.7 6.3 reshape.438
  88.0 3.5 copy.411
  95.5 11.8 %all-to-all-start.1 = ((f32[32,1,2048]{2,1,0:T(1,128)}), f32[32,1,2048]{2,1,0:T(1,128)S(1)}, u32[]{:S(2)}, u32[]{:S(2)}) async-start(f32[32,1,2048]{2,1,0:T(1,128)} %reshape.439), calls=%async_computation.1 | async-start | bytes 524288 | tf_op jit(solution)/shard_map/all_to_all | solution.py:51
  110.7 8.5 %all-to-all-done.1 = f32[32,1,2048]{2,1,0:T(1,128)S(1)} async-done(((f32[32,1,2048]{2,1,0:T(1,128)}), f32[32,1,2048]{2,1,0:T(1,128)S(1)}, u32[]{:S(2)}, u32[]{:S(2)}) %all-to-all-start.1) | async-done | bytes 262176 | tf_op jit(solution)/shard_map/all_to_all | solution.py:51
  119.2 7.4 %all-to-all-start.6 = ((f32[2,4,8,1024]{3,1,0,2:T(4,128)}), f32[2,4,8,1024]{3,1,0,2:T(4,128)S(1)}, u32[]{:S(2)}, u32[]{:S(2)}) async-start(f32[2,4,8,1024]{3,1,0,2:T(4,128)} %reshape.424), calls=%async_computation.6 | async-start | bytes 524288 | tf_op jit(solution)/shard_map/all_to_all | solution.py:50
  130.3 5.1 all-to-all-done.6
  135.4 4.8 all-to-all-start.2
  141.7 5.0 copy.421
  146.6 9.3 %reshape.435 = bf16[8,2,4096]{2,1,0:T(2,128)(2,1)} reshape(bf16[8192,1,2,4]{3,2,1,0:T(2,128)(2,1)} %bitcast.299) | data formatting | bytes 262144
  156.0 5.1 all-to-all-start.7
  162.4 5.0 copy.415
  167.4 9.3 %reshape.441 = bf16[8,2,4096]{2,1,0:T(2,128)(2,1)} reshape(bf16[8192,1,2,4]{3,2,1,0:T(2,128)(2,1)} %bitcast.300) | data formatting | bytes 262144
  176.7 5.1 all-to-all-start.3
  182.5 10.0 %reshape.436 = bf16[8192,1,2,4]{3,2,1,0:T(2,128)(2,1)} reshape(bf16[8,2,4096]{2,1,0:T(2,128)(2,1)S(1)} %all-to-all-done.7) | data formatting | bytes 262144
  192.6 8.6 %copy.358 = bf16[2,4,1,8192]{3,1,0,2:T(4,128)(2,1)S(1)} copy(bf16[2,4,1,8192]{1,0,2,3:T(2,128)(2,1)} %bitcast.301) | data formatting | bytes 262144 | tf_op jit(solution)/shard_map/all_to_all | solution.py:62
  203.3 10.1 %reshape.442 = bf16[8192,1,2,4]{3,2,1,0:T(2,128)(2,1)} reshape(bf16[8,2,4096]{2,1,0:T(2,128)(2,1)S(1)} %all-to-all-done.3) | data formatting | bytes 262144
  213.4 8.6 %copy.344 = bf16[2,4,1,8192]{3,1,2,0:T(4,128)(2,1)S(1)} copy(bf16[2,4,1,8192]{1,0,2,3:T(2,128)(2,1)} %bitcast.302) | data formatting | bytes 262144 | tf_op jit(solution)/shard_map/all_to_all | solution.py:62
  222.2 7.4 %copy.396 = bf16[1,8,8,4,256]{1,0,4,3,2:T(2,128)(2,1)} copy(bf16[1,8,8,4,256]{4,3,2,1,0:T(4,128)(2,1)S(1)} %convert_element_type.199) | data formatting | bytes 262144 | tf_op jit(solution)/shard_map/convert_element_type | solution.py:109
  230.9 4.0 collective-permute-start
  236.5 4.4 collective-permute-start.6
  243.7 3.6 collective-permute-start.2
  254.5 4.8 copy.361
  263.3 4.6 copy.347
  269.0 9.1 %multiply_convert_fusion.1 = (bf16[8,4,8,33,16]{4,2,3,1,0:T(8,128)(2,1)}, f32[8,4,8,33,16]{4,2,3,1,0:T(8,128)S(1)}) fusion(pred[8,33]{0,1:T(8,128)(4,1)S(1)} %copy-done.15, bf16[16,8,3,3,3]{0,1,4,3,2:T(8,128)(2,1)S(1)} %copy-done, bf16[8,10,6,1,7,2]{0,4,5,2,1,3:T(8,128)(2,1)S(1)} %copy-done.8, bf16[8,10,6,1,8,33]{0,4,5,2,1,3:T(8,128)(2,1)} %copy.361), kind=kOutput, calls=%fused_computation.16 | convolution fusion | flops 60009984 | bytes 1085064 | tf_op jit(solution)/shard_map/conv_general_dilated | solution.py:73
  278.2 9.5 %multiply_convert_fusion = bf16[8,4,8,33,16]{4,2,3,1,0:T(8,128)(2,1)} fusion(f32[8,4,8,33,16]{4,2,3,1,0:T(8,128)S(1)} %get-tuple-element.36, bf16[8,16,3,3,3]{1,0,4,3,2:T(8,128)(2,1)S(1)} %copy-done.14, bf16[8,10,6,1,7,2]{0,4,5,2,1,3:T(8,128)(2,1)S(1)} %slice.86, bf16[8,10,6,1,8,33]{0,4,5,2,1,3:T(8,128)(2,1)S(1)} %copy-done.2, pred[8,33]{0,1:T(8,128)(4,1)S(1)} %copy-done.15), kind=kOutput, calls=%fused_computation.15 | convolution fusion | flops 60685824 | bytes 1085064 | tf_op jit(solution)/shard_map/conv_general_dilated | solution.py:73
  287.7 3.7 copy.363
  296.9 5.2 collective-permute-start.12
  306.7 4.0 collective-permute-start.8
  312.5 4.8 copy.442
  320.3 4.5 collective-permute-start.10
  326.7 4.0 fusion.33
  330.7 3.5 copy.441
  340.1 4.7 copy.368
  345.9 9.1 %broadcast_select_fusion = f32[8,4,8,33,8]{4,2,3,1,0:T(8,128)} fusion(pred[8,33]{0,1:T(8,128)(4,1)S(1)} %copy-done.15, bf16[16,8,3,3,3]{0,1,4,3,2:T(8,128)(2,1)S(1)} %copy-done, bf16[16,10,6,1,7,2]{0,4,5,2,1,3:T(8,128)(2,1)S(1)} %slice.97, bf16[16,10,6,1,8,33]{0,4,5,2,1,3:T(8,128)(2,1)} %copy.368), kind=kOutput, calls=%fused_computation.41 | convolution fusion | flops 60072960 | bytes 811272 | tf_op jit(solution)/shard_map/conv_general_dilated | solution.py:73
  355.0 3.5 copy.369
  361.5 6.9 reshape.443
  368.4 37.0 %all-to-all-start.8 = ((f32[32,1,2048]{2,1,0:T(1,128)}), f32[32,1,2048]{2,1,0:T(1,128)S(1)}, u32[]{:S(2)}, u32[]{:S(2)}) async-start(f32[32,1,2048]{2,1,0:T(1,128)} %reshape.443), calls=%async_computation.8 | async-start | bytes 524288 | tf_op jit(solution)/shard_map/all_to_all | solution.py:47
  405.4 3.9 fusion.35
  409.3 3.7 copy.391
  414.7 4.5 copy.388
  420.6 3.9 collective-permute-start.14
  427.8 6.4 reshape.444
  434.2 3.7 copy.436
  437.8 5.4 convolution_bitcast_fusion.5
  446.6 12.3 %all-to-all-start.9 = ((f32[32,1,2048]{2,1,0:T(1,128)}), f32[32,1,2048]{2,1,0:T(1,128)S(1)}, u32[]{:S(2)}, u32[]{:S(2)}) async-start(f32[32,1,2048]{2,1,0:T(1,128)} %reshape.445), calls=%async_computation.9 | async-start | bytes 524288 | tf_op jit(solution)/shard_map/all_to_all | solution.py:51
  458.9 22.9 %fusion.52 = f32[16,8,3,3,3]{0,1,4,3,2:T(8,128)} fusion(bf16[8,4,8,33,16]{4,2,3,1,0:T(8,128)(2,1)S(1)} %copy-done.5, pred[8,33]{0,1:T(8,128)(4,1)S(1)} %copy-done.15, bf16[8,10,6,8,33,1]{3,0,5,4,2,1:T(8,128)(2,1)} %fusion.33, bf16[8,10,6,8,33,1]{3,0,5,4,2,1:T(8,128)(2,1)} %copy.388, bf16[8,10,6,8,33,1]{3,0,5,4,2,1:T(8,128)(2,1)} %fusion.35), kind=kOutput, calls=%fused_computation.59 | convolution fusion | flops 59288064 | bytes 1044744 | tf_op jit(solution)/shard_map/transpose | solution.py:92
  482.8 12.0 %copy.395 = bf16[1,16,10,6,256]{1,0,4,3,2:T(2,128)(2,1)} copy(bf16[1,16,10,6,256]{4,1,3,2,0:T(8,128)(2,1)S(1)} %pad_maximum_fusion.7) | data formatting | bytes 983040 | tf_op jit(solution)/shard_map/concatenate | solution.py:21
  498.6 5.5 all-to-all-start.10
  504.1 90.1 %fusion.123 = f32[8,16,3,3,3]{1,0,4,3,2:T(8,128)S(1)} fusion(bf16[1,16,10,6,256]{1,0,4,3,2:T(2,128)(2,1)} %copy.395, bf16[1,8,8,4,256]{1,0,4,3,2:T(2,128)(2,1)} %copy.396), kind=kOutput, calls=%fused_computation.182 | convolution fusion | flops 56475648 | bytes 636416 | tf_op jit(solution)/shard_map/transpose | solution.py:92
  594.2 82.3 %all-reduce = (f32[16,8,3,3,3]{0,1,4,3,2:T(8,128)S(1)}, f32[8,16,3,3,3]{1,0,4,3,2:T(8,128)S(1)}) all-reduce(f32[16,8,3,3,3]{0,1,4,3,2:T(8,128)S(1)} %copy-done.11, f32[8,16,3,3,3]{1,0,4,3,2:T(8,128)S(1)} %fusion.123), channel_id=1, replica_groups=mesh['gy'=32,'gz'=8] {'gy','gz'}, use_global_device_ids=true, to_apply=%region_0.1 | all-reduce | flops 6912 | bytes 55296 | tf_op jit(solution)/shard_map/psum | solution.py:123
  677.9 5.0 copy.428
  682.8 9.3 %reshape.447 = bf16[8,2,4096]{2,1,0:T(2,128)(2,1)} reshape(bf16[8192,1,2,4]{3,2,1,0:T(2,128)(2,1)} %bitcast.304) | data formatting | bytes 262144
  692.1 4.0 all-to-all-start.11
  696.8 5.2 all-to-all-done.11
  701.9 10.0 %reshape.448 = bf16[8192,1,2,4]{3,2,1,0:T(2,128)(2,1)} reshape(bf16[8,2,4096]{2,1,0:T(2,128)(2,1)S(1)} %all-to-all-done.11) | data formatting | bytes 262144
  712.0 9.6 %copy.381 = f32[2,4,8,4,256]{4,3,2,1,0:T(4,128)S(1)} copy(bf16[2,4,8,4,256]{1,0,4,3,2:T(2,128)(2,1)} %bitcast.305) | data formatting | bytes 393216 | tf_op jit(solution)/shard_map/convert_element_type | solution.py:64
  (172 shorter events, 93.0 us)
Async XLA Ops:
  0.6 268.4 %copy-start = (bf16[16,8,3,3,3]{0,1,4,3,2:T(8,128)(2,1)S(1)}, bf16[16,8,3,3,3]{0,1,4,3,2:T(8,128)(2,1)}, u32[]{:S(2)}) copy-start(bf16[16,8,3,3,3]{0,1,4,3,2:T(8,128)(2,1)} %param.8) | copy-start | bytes 20740
  0.6 25.9 %copy-start.6 = (f32[2,4,8,4,256]{4,3,2,1,0:T(4,128)S(1)}, f32[2,4,8,4,256]{4,3,2,1,0:T(4,128)}, u32[]{:S(2)}) copy-start(f32[2,4,8,4,256]{4,3,2,1,0:T(4,128)} %param.7) | copy-start | bytes 786436
  12.1 26.5 %all-to-all-start.4 = ((f32[32,1,2048]{2,1,0:T(1,128)}), f32[32,1,2048]{2,1,0:T(1,128)S(1)}, u32[]{:S(2)}, u32[]{:S(2)}) async-start(f32[32,1,2048]{2,1,0:T(1,128)} %reshape.431), calls=%async_computation.4 | async-start | bytes 524288 | tf_op jit(solution)/shard_map/all_to_all | solution.py:47
  38.5 29.9 %all-to-all-start = ((f32[32,1,2048]{2,1,0:T(1,128)}), f32[32,1,2048]{2,1,0:T(1,128)S(1)}, u32[]{:S(2)}, u32[]{:S(2)}) async-start(f32[32,1,2048]{2,1,0:T(1,128)} %reshape.437), calls=%async_computation | async-start | bytes 524288 | tf_op jit(solution)/shard_map/all_to_all | solution.py:47
  68.4 27.1 %all-to-all-start.5 = ((f32[32,1,2048]{2,1,0:T(1,128)}), f32[32,1,2048]{2,1,0:T(1,128)S(1)}, u32[]{:S(2)}, u32[]{:S(2)}) async-start(f32[32,1,2048]{2,1,0:T(1,128)} %reshape.433), calls=%async_computation.5 | async-start | bytes 524288 | tf_op jit(solution)/shard_map/all_to_all | solution.py:51
  95.5 23.8 %all-to-all-start.1 = ((f32[32,1,2048]{2,1,0:T(1,128)}), f32[32,1,2048]{2,1,0:T(1,128)S(1)}, u32[]{:S(2)}, u32[]{:S(2)}) async-start(f32[32,1,2048]{2,1,0:T(1,128)} %reshape.439), calls=%async_computation.1 | async-start | bytes 524288 | tf_op jit(solution)/shard_map/all_to_all | solution.py:51
  119.2 16.2 %all-to-all-start.6 = ((f32[2,4,8,1024]{3,1,0,2:T(4,128)}), f32[2,4,8,1024]{3,1,0,2:T(4,128)S(1)}, u32[]{:S(2)}, u32[]{:S(2)}) async-start(f32[2,4,8,1024]{3,1,0,2:T(4,128)} %reshape.424), calls=%async_computation.6 | async-start | bytes 524288 | tf_op jit(solution)/shard_map/all_to_all | solution.py:50
  135.4 20.6 %all-to-all-start.2 = ((f32[2,4,8,1024]{3,1,0,2:T(4,128)}), f32[2,4,8,1024]{3,1,0,2:T(4,128)S(1)}, u32[]{:S(2)}, u32[]{:S(2)}) async-start(f32[2,4,8,1024]{3,1,0,2:T(4,128)} %reshape.422), calls=%async_computation.2 | async-start | bytes 524288 | tf_op jit(solution)/shard_map/all_to_all | solution.py:50
  156.0 20.8 %all-to-all-start.7 = ((bf16[8,2,4096]{2,1,0:T(2,128)(2,1)}), bf16[8,2,4096]{2,1,0:T(2,128)(2,1)S(1)}, u32[]{:S(2)}, u32[]{:S(2)}) async-start(bf16[8,2,4096]{2,1,0:T(2,128)(2,1)} %reshape.435), calls=%async_computation.7 | async-start | bytes 262144 | tf_op jit(solution)/shard_map/all_to_all | solution.py:62
  162.4 19.4 %copy-start.13 = (s32[8,4]{0,1:T(4,128)S(1)}, s32[8,4]{0,1:T(4,128)}, u32[]{:S(2)}) copy-start(s32[8,4]{0,1:T(4,128)} %param.11) | copy-start | bytes 388
  176.7 26.5 %all-to-all-start.3 = ((bf16[8,2,4096]{2,1,0:T(2,128)(2,1)}), bf16[8,2,4096]{2,1,0:T(2,128)(2,1)S(1)}, u32[]{:S(2)}, u32[]{:S(2)}) async-start(bf16[8,2,4096]{2,1,0:T(2,128)(2,1)} %reshape.441), calls=%async_computation.3 | async-start | bytes 262144 | tf_op jit(solution)/shard_map/all_to_all | solution.py:62
  201.4 34.8 %collective-permute-start.4 = (bf16[1,8,1,4,256]{4,3,2,1,0:T(4,128)(2,1)S(1)}, bf16[1,8,1,4,256]{4,3,2,1,0:T(4,128)(2,1)S(1)}, u32[]{:S(2)}, u32[]{:S(2)}) collective-permute-start(bf16[1,8,1,4,256]{4,3,2,1,0:T(4,128)(2,1)S(1)} %get-tuple-element.30), channel_id=1, source_target_pairs={{0,8},{8,16},{16,24},{24,32},{32,40},{40,48},{48,56},{56,64},{64,7... | collective-permute-start | bytes 49160 | tf_op jit(solution)/shard_map/ppermute | solution.py:19
  229.6 6.7 collective-permute-start.5
  230.9 11.9 %collective-permute-start = (bf16[1,8,1,4,256]{4,3,2,1,0:T(4,128)(2,1)S(1)}, bf16[1,8,1,4,256]{4,3,2,1,0:T(4,128)(2,1)S(1)}, u32[]{:S(2)}, u32[]{:S(2)}) collective-permute-start(bf16[1,8,1,4,256]{4,3,2,1,0:T(4,128)(2,1)S(1)} %get-tuple-element.28), channel_id=1, source_target_pairs={{0,8},{8,16},{16,24},{24,32},{32,40},{40,48},{48,56},{56,64},{64,7... | collective-permute-start | bytes 49160 | tf_op jit(solution)/shard_map/ppermute | solution.py:19
  234.9 8.0 %collective-permute-start.1 = (bf16[1,8,1,4,256]{4,3,2,1,0:T(4,128)(2,1)S(1)}, bf16[1,8,1,4,256]{4,3,2,1,0:T(4,128)(2,1)S(1)}, u32[]{:S(2)}, u32[]{:S(2)}) collective-permute-start(bf16[1,8,1,4,256]{4,3,2,1,0:T(4,128)(2,1)S(1)} %get-tuple-element.27), channel_id=1, source_target_pairs={{8,0},{16,8},{24,16},{32,24},{40,32},{48,40},{56,48},{64,56},{72,6... | collective-permute-start | bytes 49160 | tf_op jit(solution)/shard_map/ppermute | solution.py:20
  236.5 12.8 %collective-permute-start.6 = (bf16[1,8,10,1,256]{4,3,2,1,0:T(2,128)(2,1)S(1)}, bf16[1,8,10,1,256]{4,3,2,1,0:T(2,128)(2,1)S(1)}, u32[]{:S(2)}, u32[]{:S(2)}) collective-permute-start(bf16[1,8,10,1,256]{4,3,2,1,0:T(2,128)(2,1)S(1)} %get-tuple-element.25), channel_id=1, source_target_pairs={{0,1},{1,2},{2,3},{3,4},{4,5},{5,6},{6,7},{8,9},{9,10},{10,11},{11... | collective-permute-start | bytes 122888 | tf_op jit(solution)/shard_map/ppermute | solution.py:19
  240.9 8.4 %collective-permute-start.7 = (bf16[1,8,10,1,256]{4,3,2,1,0:T(2,128)(2,1)S(1)}, bf16[1,8,10,1,256]{4,3,2,1,0:T(2,128)(2,1)S(1)}, u32[]{:S(2)}, u32[]{:S(2)}) collective-permute-start(bf16[1,8,10,1,256]{4,3,2,1,0:T(2,128)(2,1)S(1)} %get-tuple-element.26), channel_id=1, source_target_pairs={{1,0},{2,1},{3,2},{4,3},{5,4},{6,5},{7,6},{9,8},{10,9},{11,10},{12... | collective-permute-start | bytes 122888 | tf_op jit(solution)/shard_map/ppermute | solution.py:20
  243.7 17.3 %collective-permute-start.2 = (bf16[1,8,10,1,256]{4,3,2,1,0:T(2,128)(2,1)}, bf16[1,8,10,1,256]{4,3,2,1,0:T(2,128)(2,1)}, u32[]{:S(2)}, u32[]{:S(2)}) collective-permute-start(bf16[1,8,10,1,256]{4,3,2,1,0:T(2,128)(2,1)} %get-tuple-element.23), channel_id=1, source_target_pairs={{0,1},{1,2},{2,3},{3,4},{4,5},{5,6},{6,7},{8,9},{9,10},{10,11},{11... | collective-permute-start | bytes 122888 | tf_op jit(solution)/shard_map/ppermute | solution.py:19
  247.3 13.7 %collective-permute-start.3 = (bf16[1,8,10,1,256]{4,3,2,1,0:T(2,128)(2,1)}, bf16[1,8,10,1,256]{4,3,2,1,0:T(2,128)(2,1)}, u32[]{:S(2)}, u32[]{:S(2)}) collective-permute-start(bf16[1,8,10,1,256]{4,3,2,1,0:T(2,128)(2,1)} %get-tuple-element.24), channel_id=1, source_target_pairs={{1,0},{2,1},{3,2},{4,3},{5,4},{6,5},{7,6},{9,8},{10,9},{11,10},{12... | collective-permute-start | bytes 122888 | tf_op jit(solution)/shard_map/ppermute | solution.py:20
  261.0 8.0 %copy-start.15 = (pred[8,33]{0,1:T(8,128)(4,1)S(1)}, pred[8,33]{0,1:T(8,128)(4,1)}, u32[]{:S(2)}) copy-start(pred[8,33]{0,1:T(8,128)(4,1)} %constant.88) | copy-start | bytes 796
  262.2 6.8 copy-start.8
  269.0 9.1 %copy-start.2 = (bf16[8,10,6,1,8,33]{0,4,5,2,1,3:T(8,128)(2,1)S(1)}, bf16[8,10,6,1,8,33]{0,4,5,2,1,3:T(8,128)(2,1)}, u32[]{:S(2)}) copy-start(bf16[8,10,6,1,8,33]{0,4,5,2,1,3:T(8,128)(2,1)} %copy.347) | copy-start | bytes 760324
  269.0 9.1 %copy-start.14 = (bf16[8,16,3,3,3]{1,0,4,3,2:T(8,128)(2,1)S(1)}, bf16[8,16,3,3,3]{1,0,4,3,2:T(8,128)(2,1)}, u32[]{:S(2)}) copy-start(bf16[8,16,3,3,3]{1,0,4,3,2:T(8,128)(2,1)} %param.9) | copy-start | bytes 20740
  296.9 122.3 %collective-permute-start.12 = (bf16[1,16,1,4,256]{4,1,3,0,2:T(8,128)(2,1)}, bf16[1,16,1,4,256]{4,1,3,0,2:T(8,128)(2,1)}, u32[]{:S(2)}, u32[]{:S(2)}) collective-permute-start(bf16[1,16,1,4,256]{4,1,3,0,2:T(8,128)(2,1)} %slice_bitcast_fusion.4), channel_id=1, source_target_pairs={{0,8},{8,16},{16,24},{24,32},{32,40},{40,48},{48,56},{56,64},{64,7... | collective-permute-start | bytes 98312 | tf_op jit(solution)/shard_map/ppermute | solution.py:19
  303.2 116.0 %collective-permute-start.13 = (bf16[1,16,1,4,256]{4,1,3,0,2:T(8,128)(2,1)}, bf16[1,16,1,4,256]{4,1,3,0,2:T(8,128)(2,1)}, u32[]{:S(2)}, u32[]{:S(2)}) collective-permute-start(bf16[1,16,1,4,256]{4,1,3,0,2:T(8,128)(2,1)} %slice_bitcast_fusion.3), channel_id=1, source_target_pairs={{8,0},{16,8},{24,16},{32,24},{40,32},{48,40},{56,48},{64,56},{72,6... | collective-permute-start | bytes 98312 | tf_op jit(solution)/shard_map/ppermute | solution.py:20
  305.2 12.1 %copy-start.4 = (bf16[8,10,6,1,7,1]{5,4,2,1,0,3:T(8,128)(2,1)S(1)}, bf16[8,10,6,1,7,1]{5,4,2,1,0,3:T(8,128)(2,1)}, u32[]{:S(2)}) copy-start(bf16[8,10,6,1,7,1]{5,4,2,1,0,3:T(8,128)(2,1)} %get-tuple-element.12) | copy-start | bytes 20164
  306.7 13.5 %collective-permute-start.8 = (bf16[1,16,1,4,256]{4,1,3,0,2:T(8,128)(2,1)S(1)}, bf16[1,16,1,4,256]{4,1,3,0,2:T(8,128)(2,1)S(1)}, u32[]{:S(2)}, u32[]{:S(2)}) collective-permute-start(bf16[1,16,1,4,256]{4,1,3,0,2:T(8,128)(2,1)S(1)} %slice_bitcast_fusion.6), channel_id=1, source_target_pairs={{0,8},{8,16},{16,24},{24,32},{32,40},{40,48},{48,56},{56,64},{64,7... | collective-permute-start | bytes 98312 | tf_op jit(solution)/shard_map/ppermute | solution.py:19
  311.2 9.1 %collective-permute-start.9 = (bf16[1,16,1,4,256]{4,1,3,2,0:T(8,128)(2,1)S(1)}, bf16[1,16,1,4,256]{4,1,3,2,0:T(8,128)(2,1)S(1)}, u32[]{:S(2)}, u32[]{:S(2)}) collective-permute-start(bf16[1,16,1,4,256]{4,1,3,2,0:T(8,128)(2,1)S(1)} %slice_bitcast_fusion.5), channel_id=1, source_target_pairs={{8,0},{16,8},{24,16},{32,24},{40,32},{48,40},{56,48},{64,56},{72,6... | collective-permute-start | bytes 98312 | tf_op jit(solution)/shard_map/ppermute | solution.py:20
  320.3 16.8 %collective-permute-start.10 = (bf16[1,16,10,1,256]{4,1,3,2,0:T(8,128)(2,1)S(1)}, bf16[1,16,10,1,256]{4,1,3,2,0:T(8,128)(2,1)S(1)}, u32[]{:S(2)}, u32[]{:S(2)}) collective-permute-start(bf16[1,16,10,1,256]{4,1,3,2,0:T(8,128)(2,1)S(1)} %get-tuple-element.17), channel_id=1, source_target_pairs={{0,1},{1,2},{2,3},{3,4},{4,5},{5,6},{6,7},{8,9},{9,10},{10,11},{11... | collective-permute-start | bytes 245768 | tf_op jit(solution)/shard_map/ppermute | solution.py:19
  324.8 12.3 %collective-permute-start.11 = (bf16[1,16,10,1,256]{4,1,3,2,0:T(8,128)(2,1)S(1)}, bf16[1,16,10,1,256]{4,1,3,2,0:T(8,128)(2,1)}, u32[]{:S(2)}, u32[]{:S(2)}) collective-permute-start(bf16[1,16,10,1,256]{4,1,3,2,0:T(8,128)(2,1)S(1)} %get-tuple-element.18), channel_id=1, source_target_pairs={{1,0},{2,1},{3,2},{4,3},{5,4},{6,5},{7,6},{9,8},{10,9},{11,10},{12... | collective-permute-start | bytes 245768 | tf_op jit(solution)/shard_map/ppermute | solution.py:20
  330.7 3.5 copy-start.3
  368.4 58.1 %all-to-all-start.8 = ((f32[32,1,2048]{2,1,0:T(1,128)}), f32[32,1,2048]{2,1,0:T(1,128)S(1)}, u32[]{:S(2)}, u32[]{:S(2)}) async-start(f32[32,1,2048]{2,1,0:T(1,128)} %reshape.443), calls=%async_computation.8 | async-start | bytes 524288 | tf_op jit(solution)/shard_map/all_to_all | solution.py:47
  420.6 61.2 %collective-permute-start.14 = (bf16[1,16,10,1,256]{4,1,3,2,0:T(8,128)(2,1)}, bf16[1,16,10,1,256]{4,1,3,2,0:T(8,128)(2,1)}, u32[]{:S(2)}, u32[]{:S(2)}) collective-permute-start(bf16[1,16,10,1,256]{4,1,3,2,0:T(8,128)(2,1)} %get-tuple-element.13), channel_id=1, source_target_pairs={{0,1},{1,2},{2,3},{3,4},{4,5},{5,6},{6,7},{8,9},{9,10},{10,11},{11... | collective-permute-start | bytes 245768 | tf_op jit(solution)/shard_map/ppermute | solution.py:19
  424.5 57.3 %collective-permute-start.15 = (bf16[1,16,10,1,256]{4,1,3,2,0:T(8,128)(2,1)}, bf16[1,16,10,1,256]{4,1,3,2,0:T(8,128)(2,1)}, u32[]{:S(2)}, u32[]{:S(2)}) collective-permute-start(bf16[1,16,10,1,256]{4,1,3,2,0:T(8,128)(2,1)} %get-tuple-element.14), channel_id=1, source_target_pairs={{1,0},{2,1},{3,2},{4,3},{5,4},{6,5},{7,6},{9,8},{10,9},{11,10},{12... | collective-permute-start | bytes 245768 | tf_op jit(solution)/shard_map/ppermute | solution.py:20
  434.2 24.7 %copy-start.5 = (bf16[8,4,8,33,16]{4,2,3,1,0:T(8,128)(2,1)S(1)}, bf16[8,4,8,33,16]{4,2,3,1,0:T(8,128)(2,1)}, u32[]{:S(2)}) copy-start(bf16[8,4,8,33,16]{4,2,3,1,0:T(8,128)(2,1)} %multiply_convert_fusion) | copy-start | bytes 811012
  446.6 48.2 %all-to-all-start.9 = ((f32[32,1,2048]{2,1,0:T(1,128)}), f32[32,1,2048]{2,1,0:T(1,128)S(1)}, u32[]{:S(2)}, u32[]{:S(2)}) async-start(f32[32,1,2048]{2,1,0:T(1,128)} %reshape.445), calls=%async_computation.9 | async-start | bytes 524288 | tf_op jit(solution)/shard_map/all_to_all | solution.py:51
  498.6 178.5 %all-to-all-start.10 = ((f32[2,4,8,1024]{3,1,0,2:T(4,128)}), f32[2,4,8,1024]{3,1,0,2:T(4,128)S(1)}, u32[]{:S(2)}, u32[]{:S(2)}) async-start(f32[2,4,8,1024]{3,1,0,2:T(4,128)} %reshape.426), calls=%async_computation.10 | async-start | bytes 524288 | tf_op jit(solution)/shard_map/all_to_all | solution.py:50
  504.1 90.1 %copy-start.11 = (f32[16,8,3,3,3]{0,1,4,3,2:T(8,128)S(1)}, f32[16,8,3,3,3]{0,1,4,3,2:T(8,128)}, u32[]{:S(2)}) copy-start(f32[16,8,3,3,3]{0,1,4,3,2:T(8,128)} %fusion.52) | copy-start | bytes 41476
  504.1 173.3 %copy-start.9 = (f32[1,2,32,32]{3,2,1,0:T(8,128)S(1)}, f32[1,2,32,32]{3,2,1,0:T(8,128)}, u32[]{:S(2)}) copy-start(f32[1,2,32,32]{3,2,1,0:T(8,128)} %get-tuple-element.31) | copy-start | bytes 24580
  504.1 173.3 %copy-start.10 = (f32[1,2,32,32]{3,2,1,0:T(8,128)S(1)}, f32[1,2,32,32]{3,2,1,0:T(8,128)}, u32[]{:S(2)}) copy-start(f32[1,2,32,32]{3,2,1,0:T(8,128)} %get-tuple-element.32) | copy-start | bytes 24580
  692.1 9.8 %all-to-all-start.11 = ((bf16[8,2,4096]{2,1,0:T(2,128)(2,1)}), bf16[8,2,4096]{2,1,0:T(2,128)(2,1)S(1)}, u32[]{:S(2)}, u32[]{:S(2)}) async-start(bf16[8,2,4096]{2,1,0:T(2,128)(2,1)} %reshape.447), calls=%async_computation.11 | async-start | bytes 262144 | tf_op jit(solution)/shard_map/all_to_all | solution.py:62
  696.1 26.4 %copy-start.1 = (bf16[16,8,3,3,3]{0,1,4,3,2:T(8,128)(2,1)S(1)}, bf16[16,8,3,3,3]{0,1,4,3,2:T(8,128)(2,1)}, u32[]{:S(2)}) copy-start(bf16[16,8,3,3,3]{0,1,4,3,2:T(8,128)(2,1)} %param.8) | copy-start | bytes 20740
  696.8 24.9 %copy-start.7 = (f32[2,4,8,4,256]{4,3,2,1,0:T(4,128)S(1)}, f32[2,4,8,4,256]{4,3,2,1,0:T(4,128)}, u32[]{:S(2)}) copy-start(f32[2,4,8,4,256]{4,3,2,1,0:T(4,128)} %param.7) | copy-start | bytes 786436
  696.8 24.9 %copy-start.12 = (f32[8,4]{1,0:T(8,128)S(1)}, f32[8,4]{1,0:T(8,128)}, u32[]{:S(2)}) copy-start(f32[8,4]{1,0:T(8,128)} %copy.333) | copy-start | bytes 388
where the time goes:
time: 732 us; the launch traced here: 723 us
  local copies, waits for them, and re-layouts  264 us (36%)
  starting transfers between devices  175 us (24%)
  matrix products  151 us (21%)
  blocking collectives  82.3 us (11%)
  other arithmetic  28 us (4%)
  waiting for transfers between devices  19.7 us (3%)
    unnamed x60, local copies, waits for them, and re-layouts  126 us
    transpose x2, matrix products, kernel_gradient(): return summed.transpose(1, 0, 2, 3, 4)  113 us
    psum x1, blocking collectives, local(): summed_in, summed_out = lax.psum((local_in, local_out), ('gy', 'gz'))  82.3 us
    all_to_all x3, starting transfers between devices, spectral(): lax.all_to_all(flattened, 'gy', split_axis=3, concat_axis=2, tiled=True)  62.5 us
    all_to_all x3, starting transfers between devices, spectral(): lax.all_to_all(transformed_y, 'gy', split_axis=2, concat_axis=3, tiled=True)  36.1 us
    ppermute x8, starting transfers between devices, extended(): before = lax.ppermute(last, axis, up)  31.5 us
    conv_general_dilated x3, matrix products, convolve(): lax.conv_general_dilated(padded, kernel, (1, 1, 1), ((0, 0), (0, 0), (1,...  27.8 us
    conv_general_dilated x12, local copies, waits for them, and re-layouts, convolve(): lax.conv_general_dilated(padded, kernel, (1, 1, 1), ((0, 0), (0, 0), (1,...  25.1 us
  transfers between devices with their start and end apart: 28, of which 4 were waited for; matrix products, arithmetic and copies ran while one was open for 49% of the time, Pallas kernels for 0%

commit v1 on v0

--- a/solution.py
+++ b/solution.py
@@ -120,7 +120,7 @@
     hidden_padded = with_rims(back_hidden)
     back_image = convolve(hidden_padded, flipped(weight_in))
     spectrum = spectral(back_image.reshape(2, coil_count, cells_y, cells_z, readout), -1.0)
-    summed_in, summed_out = lax.psum((local_in, local_out), ("gy", "gz"))
+    summed_in, summed_out = lax.psum(lax.psum((local_in, local_out), "gz"), "gy")
     scale = 1.0 / math.sqrt(voxels)
     mask_field = sampling_mask.astype(jnp.float32)[None, None, :, :, None]
     grad_kspace = cotangent - consistency_weight[0] * mask_field * cotangent + spectrum

time: 732 us -> 906 us (1.24)
  blocking collectives: 82.3 us -> 227 us
  starting transfers between devices: 175 us -> 206 us
    psum x1 -> x2, blocking collectives: 82.3 us -> 227 us  [the longest x1 199 us: local(): lax.psum(lax.psum((local_in, local_out), 'gz'), 'gy')]
    all_to_all x3, starting transfers between devices: 14.2 us -> 45.1 us  [spectral(): lax.all_to_all(as_sent(transformed_z), 'gz', split_axis=3, concat_axis=2,...]
  transfers between devices with their start and end apart: 28 -> 28, of which waited for: 4 -> 4; matrix products, arithmetic and copies ran while one was open for 49% -> 40% of each run, Pallas kernels for 0% -> 0%
where the time goes in v1:
time: 906 us; the launch traced here: 898 us
  local copies, waits for them, and re-layouts  264 us (29%)
  blocking collectives  227 us (25%)
  starting transfers between devices  206 us (23%)
  matrix products  152 us (17%)
  other arithmetic  27.7 us (3%)
  waiting for transfers between devices  19.8 us (2%)
    psum x1, blocking collectives, local(): lax.psum(lax.psum((local_in, local_out), 'gz'), 'gy')  199 us
    unnamed x60, local copies, waits for them, and re-layouts  126 us
    transpose x2, matrix products, kernel_gradient(): return summed.transpose(1, 0, 2, 3, 4)  113 us
    all_to_all x3, starting transfers between devices, spectral(): lax.all_to_all(flattened, 'gy', split_axis=3, concat_axis=2, tiled=True)  62.5 us
    all_to_all x3, starting transfers between devices, spectral(): lax.all_to_all(as_sent(transformed_z), 'gz', split_axis=3, concat_axis=2,...  45.1 us
    all_to_all x3, starting transfers between devices, spectral(): lax.all_to_all(transformed_y, 'gy', split_axis=2, concat_axis=3, tiled=True)  36.1 us
    ppermute x8, starting transfers between devices, extended(): before = lax.ppermute(last, axis, up)  31.5 us
    psum x1, blocking collectives, local(): lax.psum((local_in, local_out), 'gz')  27.9 us
  transfers between devices with their start and end apart: 28, of which 4 were waited for; matrix products, arithmetic and copies ran while one was open for 40% of the time, Pallas kernels for 0%

profile of v1, /device:TPU:1, one launch (start us, length us, event | category | flops | bytes accessed | tf_op | source)
XLA Modules:
  0.0 897.6 jit_solution(4311568694224994343)
XLA Ops:
  0.7 4.5 copy.348
  5.1 6.9 reshape.431
  12.0 14.5 %all-to-all-start.4 = ((f32[32,1,2048]{2,1,0:T(1,128)}), f32[32,1,2048]{2,1,0:T(1,128)S(1)}, u32[]{:S(2)}, u32[]{:S(2)}) async-start(f32[32,1,2048]{2,1,0:T(1,128)} %reshape.431), calls=%async_computation.4 | async-start | bytes 524288 | tf_op jit(solution)/shard_map/all_to_all | solution.py:47
  29.7 6.9 reshape.437
  38.5 11.0 %all-to-all-start = ((f32[32,1,2048]{2,1,0:T(1,128)}), f32[32,1,2048]{2,1,0:T(1,128)S(1)}, u32[]{:S(2)}, u32[]{:S(2)}) async-start(f32[32,1,2048]{2,1,0:T(1,128)} %reshape.437), calls=%async_computation | async-start | bytes 524288 | tf_op jit(solution)/shard_map/all_to_all | solution.py:47
  54.5 6.3 reshape.432
  60.9 3.5 copy.417
  68.3 12.0 %all-to-all-start.5 = ((f32[32,1,2048]{2,1,0:T(1,128)}), f32[32,1,2048]{2,1,0:T(1,128)S(1)}, u32[]{:S(2)}, u32[]{:S(2)}) async-start(f32[32,1,2048]{2,1,0:T(1,128)} %reshape.433), calls=%async_computation.5 | async-start | bytes 524288 | tf_op jit(solution)/shard_map/all_to_all | solution.py:51
  81.5 6.3 reshape.438
  87.9 3.5 copy.411
  95.3 11.8 %all-to-all-start.1 = ((f32[32,1,2048]{2,1,0:T(1,128)}), f32[32,1,2048]{2,1,0:T(1,128)S(1)}, u32[]{:S(2)}, u32[]{:S(2)}) async-start(f32[32,1,2048]{2,1,0:T(1,128)} %reshape.439), calls=%async_computation.1 | async-start | bytes 524288 | tf_op jit(solution)/shard_map/all_to_all | solution.py:51
  110.5 8.6 all-to-all-done.1
  119.1 7.4 all-to-all-start.6
  130.1 5.2 all-to-all-done.6
  135.2 4.8 all-to-all-start.2
  141.5 4.9 copy.421
  146.4 9.3 %reshape.435 = bf16[8,2,4096]{2,1,0:T(2,128)(2,1)} reshape(bf16[8192,1,2,4]{3,2,1,0:T(2,128)(2,1)} %bitcast.299) | data formatting | bytes 262144
  155.8 5.1 all-to-all-start.7
  162.2 4.9 copy.415
  167.1 9.3 %reshape.441 = bf16[8,2,4096]{2,1,0:T(2,128)(2,1)} reshape(bf16[8192,1,2,4]{3,2,1,0:T(2,128)(2,1)} %bitcast.300) | data formatting | bytes 262144
  176.5 5.1 all-to-all-start.3
  182.3 10.0 %reshape.436 = bf16[8192,1,2,4]{3,2,1,0:T(2,128)(2,1)} reshape(bf16[8,2,4096]{2,1,0:T(2,128)(2,1)S(1)} %all-to-all-done.7) | data formatting | bytes 262144
  192.3 8.6 copy.358
  203.0 10.0 %reshape.442 = bf16[8192,1,2,4]{3,2,1,0:T(2,128)(2,1)} reshape(bf16[8,2,4096]{2,1,0:T(2,128)(2,1)S(1)} %all-to-all-done.3) | data formatting | bytes 262144
  213.0 8.6 copy.344
  221.9 7.4 copy.396
  230.6 4.0 collective-permute-start
  236.1 4.4 collective-permute-start.6
  243.3 3.6 collective-permute-start.2
  254.2 4.8 copy.361
  262.9 4.6 copy.347
  268.7 9.1 %multiply_convert_fusion.1 = (bf16[8,4,8,33,16]{4,2,3,1,0:T(8,128)(2,1)}, f32[8,4,8,33,16]{4,2,3,1,0:T(8,128)S(1)}) fusion(pred[8,33]{0,1:T(8,128)(4,1)S(1)} %copy-done.15, bf16[16,8,3,3,3]{0,1,4,3,2:T(8,128)(2,1)S(1)} %copy-done, bf16[8,10,6,1,7,2]{0,4,5,2,1,3:T(8,128)(2,1)S(1)} %copy-done.8, bf16[8,10,6,1,8,33]{0,4,5,2,1,3:T(8,128)(2,1)} %copy.361), kind=kOutput, calls=%fused_computation.16 | convolution fusion | flops 60009984 | bytes 1085064 | tf_op jit(solution)/shard_map/conv_general_dilated | solution.py:73
  277.8 9.5 %multiply_convert_fusion = bf16[8,4,8,33,16]{4,2,3,1,0:T(8,128)(2,1)} fusion(f32[8,4,8,33,16]{4,2,3,1,0:T(8,128)S(1)} %get-tuple-element.38, bf16[8,16,3,3,3]{1,0,4,3,2:T(8,128)(2,1)S(1)} %copy-done.14, bf16[8,10,6,1,7,2]{0,4,5,2,1,3:T(8,128)(2,1)S(1)} %slice.86, bf16[8,10,6,1,8,33]{0,4,5,2,1,3:T(8,128)(2,1)S(1)} %copy-done.2, pred[8,33]{0,1:T(8,128)(4,1)S(1)} %copy-done.15), kind=kOutput, calls=%fused_computation.15 | convolution fusion | flops 60685824 | bytes 1085064 | tf_op jit(solution)/shard_map/conv_general_dilated | solution.py:73
  287.3 3.7 copy.363
  296.5 5.3 collective-permute-start.12
  306.4 4.0 collective-permute-start.8
  312.1 4.8 copy.442
  319.9 4.5 collective-permute-start.10
  326.3 4.0 fusion.33
  330.3 3.5 copy.441
  339.8 4.8 copy.368
  345.6 9.1 %broadcast_select_fusion = f32[8,4,8,33,8]{4,2,3,1,0:T(8,128)} fusion(pred[8,33]{0,1:T(8,128)(4,1)S(1)} %copy-done.15, bf16[16,8,3,3,3]{0,1,4,3,2:T(8,128)(2,1)S(1)} %copy-done, bf16[16,10,6,1,7,2]{0,4,5,2,1,3:T(8,128)(2,1)S(1)} %slice.97, bf16[16,10,6,1,8,33]{0,4,5,2,1,3:T(8,128)(2,1)} %copy.368), kind=kOutput, calls=%fused_computation.41 | convolution fusion | flops 60072960 | bytes 811272 | tf_op jit(solution)/shard_map/conv_general_dilated | solution.py:73
  361.2 6.9 reshape.443
  368.1 37.0 %all-to-all-start.8 = ((f32[32,1,2048]{2,1,0:T(1,128)}), f32[32,1,2048]{2,1,0:T(1,128)S(1)}, u32[]{:S(2)}, u32[]{:S(2)}) async-start(f32[32,1,2048]{2,1,0:T(1,128)} %reshape.443), calls=%async_computation.8 | async-start | bytes 524288 | tf_op jit(solution)/shard_map/all_to_all | solution.py:47
  405.1 3.9 fusion.35
  409.0 3.7 copy.391
  414.4 4.5 copy.388
  420.4 3.9 collective-permute-start.14
  427.5 6.4 reshape.444
  433.9 3.7 copy.436
  437.5 5.4 convolution_bitcast_fusion.5
  446.3 12.3 %all-to-all-start.9 = ((f32[32,1,2048]{2,1,0:T(1,128)}), f32[32,1,2048]{2,1,0:T(1,128)S(1)}, u32[]{:S(2)}, u32[]{:S(2)}) async-start(f32[32,1,2048]{2,1,0:T(1,128)} %reshape.445), calls=%async_computation.9 | async-start | bytes 524288 | tf_op jit(solution)/shard_map/all_to_all | solution.py:51
  458.6 22.9 %fusion.52 = f32[16,8,3,3,3]{0,1,4,3,2:T(8,128)} fusion(bf16[8,4,8,33,16]{4,2,3,1,0:T(8,128)(2,1)S(1)} %copy-done.5, pred[8,33]{0,1:T(8,128)(4,1)S(1)} %copy-done.15, bf16[8,10,6,8,33,1]{3,0,5,4,2,1:T(8,128)(2,1)} %fusion.33, bf16[8,10,6,8,33,1]{3,0,5,4,2,1:T(8,128)(2,1)} %copy.388, bf16[8,10,6,8,33,1]{3,0,5,4,2,1:T(8,128)(2,1)} %fusion.35), kind=kOutput, calls=%fused_computation.59 | convolution fusion | flops 59288064 | bytes 1044744 | tf_op jit(solution)/shard_map/transpose | solution.py:92
  482.5 11.9 %copy.395 = bf16[1,16,10,6,256]{1,0,4,3,2:T(2,128)(2,1)} copy(bf16[1,16,10,6,256]{4,1,3,2,0:T(8,128)(2,1)S(1)} %pad_maximum_fusion.7) | data formatting | bytes 983040 | tf_op jit(solution)/shard_map/concatenate | solution.py:21
  498.2 5.5 all-to-all-start.10
  503.7 90.1 %fusion.123 = f32[8,16,3,3,3]{1,0,4,3,2:T(8,128)S(1)} fusion(bf16[1,16,10,6,256]{1,0,4,3,2:T(2,128)(2,1)} %copy.395, bf16[1,8,8,4,256]{1,0,4,3,2:T(2,128)(2,1)} %copy.396), kind=kOutput, calls=%fused_computation.182 | convolution fusion | flops 56475648 | bytes 636416 | tf_op jit(solution)/shard_map/transpose | solution.py:92
  593.8 27.9 %all-reduce.1 = (f32[16,8,3,3,3]{0,1,4,3,2:T(8,128)S(1)}, f32[8,16,3,3,3]{1,0,4,3,2:T(8,128)S(1)}) all-reduce(f32[16,8,3,3,3]{0,1,4,3,2:T(8,128)S(1)} %copy-done.11, f32[8,16,3,3,3]{1,0,4,3,2:T(8,128)S(1)} %fusion.123), channel_id=1, replica_groups=mesh['gy'=32,'gz'=8] {'gz'}, use_global_device_ids=true, to_apply=%region_0.1 | all-reduce | flops 6912 | bytes 55296 | tf_op jit(solution)/shard_map/psum | solution.py:123
  621.7 198.9 %all-reduce = (f32[16,8,3,3,3]{0,1,4,3,2:T(8,128)S(1)}, f32[8,16,3,3,3]{1,0,4,3,2:T(8,128)S(1)}) all-reduce(f32[16,8,3,3,3]{0,1,4,3,2:T(8,128)S(1)} %get-tuple-element.5, f32[8,16,3,3,3]{1,0,4,3,2:T(8,128)S(1)} %get-tuple-element.6), channel_id=1, replica_groups=mesh['gy'=32,'gz'=8] {'gy'}, use_global_device_ids=true, to_apply=%region_1.2 | all-reduce | flops 6912 | bytes 55296 | tf_op jit(solution)/shard_map/psum | solution.py:123
  821.9 5.0 copy.428
  826.9 9.3 %reshape.447 = bf16[8,2,4096]{2,1,0:T(2,128)(2,1)} reshape(bf16[8192,1,2,4]{3,2,1,0:T(2,128)(2,1)} %bitcast.304) | data formatting | bytes 262144
  836.2 34.9 %all-to-all-start.11 = ((bf16[8,2,4096]{2,1,0:T(2,128)(2,1)}), bf16[8,2,4096]{2,1,0:T(2,128)(2,1)S(1)}, u32[]{:S(2)}, u32[]{:S(2)}) async-start(bf16[8,2,4096]{2,1,0:T(2,128)(2,1)} %reshape.447), calls=%async_computation.11 | async-start | bytes 262144 | tf_op jit(solution)/shard_map/all_to_all | solution.py:62
  871.7 5.2 all-to-all-done.11
  876.9 10.0 %reshape.448 = bf16[8192,1,2,4]{3,2,1,0:T(2,128)(2,1)} reshape(bf16[8,2,4096]{2,1,0:T(2,128)(2,1)S(1)} %all-to-all-done.11) | data formatting | bytes 262144
  886.9 9.6 %copy.381 = f32[2,4,8,4,256]{4,3,2,1,0:T(4,128)S(1)} copy(bf16[2,4,8,4,256]{1,0,4,3,2:T(2,128)(2,1)} %bitcast.305) | data formatting | bytes 393216 | tf_op jit(solution)/shard_map/convert_element_type | solution.py:64
  (173 shorter events, 96.1 us)
Async XLA Ops:
  0.6 268.0 %copy-start = (bf16[16,8,3,3,3]{0,1,4,3,2:T(8,128)(2,1)S(1)}, bf16[16,8,3,3,3]{0,1,4,3,2:T(8,128)(2,1)}, u32[]{:S(2)}) copy-start(bf16[16,8,3,3,3]{0,1,4,3,2:T(8,128)(2,1)} %param.8) | copy-start | bytes 20740
  0.6 25.9 %copy-start.6 = (f32[2,4,8,4,256]{4,3,2,1,0:T(4,128)S(1)}, f32[2,4,8,4,256]{4,3,2,1,0:T(4,128)}, u32[]{:S(2)}) copy-start(f32[2,4,8,4,256]{4,3,2,1,0:T(4,128)} %param.7) | copy-start | bytes 786436
  12.0 26.5 %all-to-all-start.4 = ((f32[32,1,2048]{2,1,0:T(1,128)}), f32[32,1,2048]{2,1,0:T(1,128)S(1)}, u32[]{:S(2)}, u32[]{:S(2)}) async-start(f32[32,1,2048]{2,1,0:T(1,128)} %reshape.431), calls=%async_computation.4 | async-start | bytes 524288 | tf_op jit(solution)/shard_map/all_to_all | solution.py:47
  38.5 29.8 %all-to-all-start = ((f32[32,1,2048]{2,1,0:T(1,128)}), f32[32,1,2048]{2,1,0:T(1,128)S(1)}, u32[]{:S(2)}, u32[]{:S(2)}) async-start(f32[32,1,2048]{2,1,0:T(1,128)} %reshape.437), calls=%async_computation | async-start | bytes 524288 | tf_op jit(solution)/shard_map/all_to_all | solution.py:47
  68.3 27.0 %all-to-all-start.5 = ((f32[32,1,2048]{2,1,0:T(1,128)}), f32[32,1,2048]{2,1,0:T(1,128)S(1)}, u32[]{:S(2)}, u32[]{:S(2)}) async-start(f32[32,1,2048]{2,1,0:T(1,128)} %reshape.433), calls=%async_computation.5 | async-start | bytes 524288 | tf_op jit(solution)/shard_map/all_to_all | solution.py:51
  95.3 23.8 %all-to-all-start.1 = ((f32[32,1,2048]{2,1,0:T(1,128)}), f32[32,1,2048]{2,1,0:T(1,128)S(1)}, u32[]{:S(2)}, u32[]{:S(2)}) async-start(f32[32,1,2048]{2,1,0:T(1,128)} %reshape.439), calls=%async_computation.1 | async-start | bytes 524288 | tf_op jit(solution)/shard_map/all_to_all | solution.py:51
  119.1 16.2 %all-to-all-start.6 = ((f32[2,4,8,1024]{3,1,0,2:T(4,128)}), f32[2,4,8,1024]{3,1,0,2:T(4,128)S(1)}, u32[]{:S(2)}, u32[]{:S(2)}) async-start(f32[2,4,8,1024]{3,1,0,2:T(4,128)} %reshape.424), calls=%async_computation.6 | async-start | bytes 524288 | tf_op jit(solution)/shard_map/all_to_all | solution.py:50
  135.2 20.5 %all-to-all-start.2 = ((f32[2,4,8,1024]{3,1,0,2:T(4,128)}), f32[2,4,8,1024]{3,1,0,2:T(4,128)S(1)}, u32[]{:S(2)}, u32[]{:S(2)}) async-start(f32[2,4,8,1024]{3,1,0,2:T(4,128)} %reshape.422), calls=%async_computation.2 | async-start | bytes 524288 | tf_op jit(solution)/shard_map/all_to_all | solution.py:50
  155.8 20.7 %all-to-all-start.7 = ((bf16[8,2,4096]{2,1,0:T(2,128)(2,1)}), bf16[8,2,4096]{2,1,0:T(2,128)(2,1)S(1)}, u32[]{:S(2)}, u32[]{:S(2)}) async-start(bf16[8,2,4096]{2,1,0:T(2,128)(2,1)} %reshape.435), calls=%async_computation.7 | async-start | bytes 262144 | tf_op jit(solution)/shard_map/all_to_all | solution.py:62
  162.2 19.4 %copy-start.13 = (s32[8,4]{0,1:T(4,128)S(1)}, s32[8,4]{0,1:T(4,128)}, u32[]{:S(2)}) copy-start(s32[8,4]{0,1:T(4,128)} %param.11) | copy-start | bytes 388
  176.5 26.5 %all-to-all-start.3 = ((bf16[8,2,4096]{2,1,0:T(2,128)(2,1)}), bf16[8,2,4096]{2,1,0:T(2,128)(2,1)S(1)}, u32[]{:S(2)}, u32[]{:S(2)}) async-start(bf16[8,2,4096]{2,1,0:T(2,128)(2,1)} %reshape.441), calls=%async_computation.3 | async-start | bytes 262144 | tf_op jit(solution)/shard_map/all_to_all | solution.py:62
  201.1 34.8 %collective-permute-start.4 = (bf16[1,8,1,4,256]{4,3,2,1,0:T(4,128)(2,1)S(1)}, bf16[1,8,1,4,256]{4,3,2,1,0:T(4,128)(2,1)S(1)}, u32[]{:S(2)}, u32[]{:S(2)}) collective-permute-start(bf16[1,8,1,4,256]{4,3,2,1,0:T(4,128)(2,1)S(1)} %get-tuple-element.32), channel_id=1, source_target_pairs={{0,8},{8,16},{16,24},{24,32},{32,40},{40,48},{48,56},{56,64},{64,7... | collective-permute-start | bytes 49160 | tf_op jit(solution)/shard_map/ppermute | solution.py:19
  229.3 6.7 collective-permute-start.5
  230.6 11.9 %collective-permute-start = (bf16[1,8,1,4,256]{4,3,2,1,0:T(4,128)(2,1)S(1)}, bf16[1,8,1,4,256]{4,3,2,1,0:T(4,128)(2,1)S(1)}, u32[]{:S(2)}, u32[]{:S(2)}) collective-permute-start(bf16[1,8,1,4,256]{4,3,2,1,0:T(4,128)(2,1)S(1)} %get-tuple-element.30), channel_id=1, source_target_pairs={{0,8},{8,16},{16,24},{24,32},{32,40},{40,48},{48,56},{56,64},{64,7... | collective-permute-start | bytes 49160 | tf_op jit(solution)/shard_map/ppermute | solution.py:19
  234.5 8.0 collective-permute-start.1
  236.1 12.8 %collective-permute-start.6 = (bf16[1,8,10,1,256]{4,3,2,1,0:T(2,128)(2,1)S(1)}, bf16[1,8,10,1,256]{4,3,2,1,0:T(2,128)(2,1)S(1)}, u32[]{:S(2)}, u32[]{:S(2)}) collective-permute-start(bf16[1,8,10,1,256]{4,3,2,1,0:T(2,128)(2,1)S(1)} %get-tuple-element.27), channel_id=1, source_target_pairs={{0,1},{1,2},{2,3},{3,4},{4,5},{5,6},{6,7},{8,9},{9,10},{10,11},{11... | collective-permute-start | bytes 122888 | tf_op jit(solution)/shard_map/ppermute | solution.py:19
  240.5 8.4 collective-permute-start.7
  243.3 17.3 %collective-permute-start.2 = (bf16[1,8,10,1,256]{4,3,2,1,0:T(2,128)(2,1)}, bf16[1,8,10,1,256]{4,3,2,1,0:T(2,128)(2,1)}, u32[]{:S(2)}, u32[]{:S(2)}) collective-permute-start(bf16[1,8,10,1,256]{4,3,2,1,0:T(2,128)(2,1)} %get-tuple-element.25), channel_id=1, source_target_pairs={{0,1},{1,2},{2,3},{3,4},{4,5},{5,6},{6,7},{8,9},{9,10},{10,11},{11... | collective-permute-start | bytes 122888 | tf_op jit(solution)/shard_map/ppermute | solution.py:19
  247.0 13.7 %collective-permute-start.3 = (bf16[1,8,10,1,256]{4,3,2,1,0:T(2,128)(2,1)}, bf16[1,8,10,1,256]{4,3,2,1,0:T(2,128)(2,1)}, u32[]{:S(2)}, u32[]{:S(2)}) collective-permute-start(bf16[1,8,10,1,256]{4,3,2,1,0:T(2,128)(2,1)} %get-tuple-element.26), channel_id=1, source_target_pairs={{1,0},{2,1},{3,2},{4,3},{5,4},{6,5},{7,6},{9,8},{10,9},{11,10},{12... | collective-permute-start | bytes 122888 | tf_op jit(solution)/shard_map/ppermute | solution.py:20
  260.6 8.0 copy-start.15
  261.9 6.8 copy-start.8
  268.6 9.1 %copy-start.2 = (bf16[8,10,6,1,8,33]{0,4,5,2,1,3:T(8,128)(2,1)S(1)}, bf16[8,10,6,1,8,33]{0,4,5,2,1,3:T(8,128)(2,1)}, u32[]{:S(2)}) copy-start(bf16[8,10,6,1,8,33]{0,4,5,2,1,3:T(8,128)(2,1)} %copy.347) | copy-start | bytes 760324
  268.6 9.1 %copy-start.14 = (bf16[8,16,3,3,3]{1,0,4,3,2:T(8,128)(2,1)S(1)}, bf16[8,16,3,3,3]{1,0,4,3,2:T(8,128)(2,1)}, u32[]{:S(2)}) copy-start(bf16[8,16,3,3,3]{1,0,4,3,2:T(8,128)(2,1)} %param.9) | copy-start | bytes 20740
  296.5 122.4 %collective-permute-start.12 = (bf16[1,16,1,4,256]{4,1,3,0,2:T(8,128)(2,1)}, bf16[1,16,1,4,256]{4,1,3,0,2:T(8,128)(2,1)}, u32[]{:S(2)}, u32[]{:S(2)}) collective-permute-start(bf16[1,16,1,4,256]{4,1,3,0,2:T(8,128)(2,1)} %slice_bitcast_fusion.4), channel_id=1, source_target_pairs={{0,8},{8,16},{16,24},{24,32},{32,40},{40,48},{48,56},{56,64},{64,7... | collective-permute-start | bytes 98312 | tf_op jit(solution)/shard_map/ppermute | solution.py:19
  302.9 116.1 %collective-permute-start.13 = (bf16[1,16,1,4,256]{4,1,3,0,2:T(8,128)(2,1)}, bf16[1,16,1,4,256]{4,1,3,0,2:T(8,128)(2,1)}, u32[]{:S(2)}, u32[]{:S(2)}) collective-permute-start(bf16[1,16,1,4,256]{4,1,3,0,2:T(8,128)(2,1)} %slice_bitcast_fusion.3), channel_id=1, source_target_pairs={{8,0},{16,8},{24,16},{32,24},{40,32},{48,40},{56,48},{64,56},{72,6... | collective-permute-start | bytes 98312 | tf_op jit(solution)/shard_map/ppermute | solution.py:20
  304.9 12.1 %copy-start.4 = (bf16[8,10,6,1,7,1]{5,4,2,1,0,3:T(8,128)(2,1)S(1)}, bf16[8,10,6,1,7,1]{5,4,2,1,0,3:T(8,128)(2,1)}, u32[]{:S(2)}) copy-start(bf16[8,10,6,1,7,1]{5,4,2,1,0,3:T(8,128)(2,1)} %get-tuple-element.14) | copy-start | bytes 20164
  306.4 13.5 %collective-permute-start.8 = (bf16[1,16,1,4,256]{4,1,3,0,2:T(8,128)(2,1)S(1)}, bf16[1,16,1,4,256]{4,1,3,0,2:T(8,128)(2,1)S(1)}, u32[]{:S(2)}, u32[]{:S(2)}) collective-permute-start(bf16[1,16,1,4,256]{4,1,3,0,2:T(8,128)(2,1)S(1)} %slice_bitcast_fusion.6), channel_id=1, source_target_pairs={{0,8},{8,16},{16,24},{24,32},{32,40},{40,48},{48,56},{56,64},{64,7... | collective-permute-start | bytes 98312 | tf_op jit(solution)/shard_map/ppermute | solution.py:19
  310.8 9.1 %collective-permute-start.9 = (bf16[1,16,1,4,256]{4,1,3,2,0:T(8,128)(2,1)S(1)}, bf16[1,16,1,4,256]{4,1,3,2,0:T(8,128)(2,1)S(1)}, u32[]{:S(2)}, u32[]{:S(2)}) collective-permute-start(bf16[1,16,1,4,256]{4,1,3,2,0:T(8,128)(2,1)S(1)} %slice_bitcast_fusion.5), channel_id=1, source_target_pairs={{8,0},{16,8},{24,16},{32,24},{40,32},{48,40},{56,48},{64,56},{72,6... | collective-permute-start | bytes 98312 | tf_op jit(solution)/shard_map/ppermute | solution.py:20
  319.9 16.9 %collective-permute-start.10 = (bf16[1,16,10,1,256]{4,1,3,2,0:T(8,128)(2,1)S(1)}, bf16[1,16,10,1,256]{4,1,3,2,0:T(8,128)(2,1)S(1)}, u32[]{:S(2)}, u32[]{:S(2)}) collective-permute-start(bf16[1,16,10,1,256]{4,1,3,2,0:T(8,128)(2,1)S(1)} %get-tuple-element.19), channel_id=1, source_target_pairs={{0,1},{1,2},{2,3},{3,4},{4,5},{5,6},{6,7},{8,9},{9,10},{10,11},{11... | collective-permute-start | bytes 245768 | tf_op jit(solution)/shard_map/ppermute | solution.py:19
  324.4 12.4 %collective-permute-start.11 = (bf16[1,16,10,1,256]{4,1,3,2,0:T(8,128)(2,1)S(1)}, bf16[1,16,10,1,256]{4,1,3,2,0:T(8,128)(2,1)}, u32[]{:S(2)}, u32[]{:S(2)}) collective-permute-start(bf16[1,16,10,1,256]{4,1,3,2,0:T(8,128)(2,1)S(1)} %get-tuple-element.20), channel_id=1, source_target_pairs={{1,0},{2,1},{3,2},{4,3},{5,4},{6,5},{7,6},{9,8},{10,9},{11,10},{12... | collective-permute-start | bytes 245768 | tf_op jit(solution)/shard_map/ppermute | solution.py:20
  330.3 3.5 copy-start.3
  368.1 58.1 %all-to-all-start.8 = ((f32[32,1,2048]{2,1,0:T(1,128)}), f32[32,1,2048]{2,1,0:T(1,128)S(1)}, u32[]{:S(2)}, u32[]{:S(2)}) async-start(f32[32,1,2048]{2,1,0:T(1,128)} %reshape.443), calls=%async_computation.8 | async-start | bytes 524288 | tf_op jit(solution)/shard_map/all_to_all | solution.py:47
  420.4 61.1 %collective-permute-start.14 = (bf16[1,16,10,1,256]{4,1,3,2,0:T(8,128)(2,1)}, bf16[1,16,10,1,256]{4,1,3,2,0:T(8,128)(2,1)}, u32[]{:S(2)}, u32[]{:S(2)}) collective-permute-start(bf16[1,16,10,1,256]{4,1,3,2,0:T(8,128)(2,1)} %get-tuple-element.15), channel_id=1, source_target_pairs={{0,1},{1,2},{2,3},{3,4},{4,5},{5,6},{6,7},{8,9},{9,10},{10,11},{11... | collective-permute-start | bytes 245768 | tf_op jit(solution)/shard_map/ppermute | solution.py:19
  424.3 57.2 %collective-permute-start.15 = (bf16[1,16,10,1,256]{4,1,3,2,0:T(8,128)(2,1)}, bf16[1,16,10,1,256]{4,1,3,2,0:T(8,128)(2,1)}, u32[]{:S(2)}, u32[]{:S(2)}) collective-permute-start(bf16[1,16,10,1,256]{4,1,3,2,0:T(8,128)(2,1)} %get-tuple-element.16), channel_id=1, source_target_pairs={{1,0},{2,1},{3,2},{4,3},{5,4},{6,5},{7,6},{9,8},{10,9},{11,10},{12... | collective-permute-start | bytes 245768 | tf_op jit(solution)/shard_map/ppermute | solution.py:20
  433.9 24.7 %copy-start.5 = (bf16[8,4,8,33,16]{4,2,3,1,0:T(8,128)(2,1)S(1)}, bf16[8,4,8,33,16]{4,2,3,1,0:T(8,128)(2,1)}, u32[]{:S(2)}) copy-start(bf16[8,4,8,33,16]{4,2,3,1,0:T(8,128)(2,1)} %multiply_convert_fusion) | copy-start | bytes 811012
  446.3 48.2 %all-to-all-start.9 = ((f32[32,1,2048]{2,1,0:T(1,128)}), f32[32,1,2048]{2,1,0:T(1,128)S(1)}, u32[]{:S(2)}, u32[]{:S(2)}) async-start(f32[32,1,2048]{2,1,0:T(1,128)} %reshape.445), calls=%async_computation.9 | async-start | bytes 524288 | tf_op jit(solution)/shard_map/all_to_all | solution.py:51
  498.2 323.0 %all-to-all-start.10 = ((f32[2,4,8,1024]{3,1,0,2:T(4,128)}), f32[2,4,8,1024]{3,1,0,2:T(4,128)S(1)}, u32[]{:S(2)}, u32[]{:S(2)}) async-start(f32[2,4,8,1024]{3,1,0,2:T(4,128)} %reshape.426), calls=%async_computation.10 | async-start | bytes 524288 | tf_op jit(solution)/shard_map/all_to_all | solution.py:50
  503.7 90.1 %copy-start.11 = (f32[16,8,3,3,3]{0,1,4,3,2:T(8,128)S(1)}, f32[16,8,3,3,3]{0,1,4,3,2:T(8,128)}, u32[]{:S(2)}) copy-start(f32[16,8,3,3,3]{0,1,4,3,2:T(8,128)} %fusion.52) | copy-start | bytes 41476
  503.7 317.8 %copy-start.9 = (f32[1,2,32,32]{3,2,1,0:T(8,128)S(1)}, f32[1,2,32,32]{3,2,1,0:T(8,128)}, u32[]{:S(2)}) copy-start(f32[1,2,32,32]{3,2,1,0:T(8,128)} %get-tuple-element.33) | copy-start | bytes 24580
  503.7 317.8 %copy-start.10 = (f32[1,2,32,32]{3,2,1,0:T(8,128)S(1)}, f32[1,2,32,32]{3,2,1,0:T(8,128)}, u32[]{:S(2)}) copy-start(f32[1,2,32,32]{3,2,1,0:T(8,128)} %get-tuple-element.34) | copy-start | bytes 24580
  836.2 40.7 %all-to-all-start.11 = ((bf16[8,2,4096]{2,1,0:T(2,128)(2,1)}), bf16[8,2,4096]{2,1,0:T(2,128)(2,1)S(1)}, u32[]{:S(2)}, u32[]{:S(2)}) async-start(bf16[8,2,4096]{2,1,0:T(2,128)(2,1)} %reshape.447), calls=%async_computation.11 | async-start | bytes 262144 | tf_op jit(solution)/shard_map/all_to_all | solution.py:62
  871.0 26.4 %copy-start.1 = (bf16[16,8,3,3,3]{0,1,4,3,2:T(8,128)(2,1)S(1)}, bf16[16,8,3,3,3]{0,1,4,3,2:T(8,128)(2,1)}, u32[]{:S(2)}) copy-start(bf16[16,8,3,3,3]{0,1,4,3,2:T(8,128)(2,1)} %param.8) | copy-start | bytes 20740
  871.7 24.8 %copy-start.7 = (f32[2,4,8,4,256]{4,3,2,1,0:T(4,128)S(1)}, f32[2,4,8,4,256]{4,3,2,1,0:T(4,128)}, u32[]{:S(2)}) copy-start(f32[2,4,8,4,256]{4,3,2,1,0:T(4,128)} %param.7) | copy-start | bytes 786436
  871.7 24.9 %copy-start.12 = (f32[8,4]{1,0:T(8,128)S(1)}, f32[8,4]{1,0:T(8,128)}, u32[]{:S(2)}) copy-start(f32[8,4]{1,0:T(8,128)} %copy.333) | copy-start | bytes 388
